TPU v7x, 256 devices: a whole 4x4x8 slice. The times are simulated.
256 devices in a mesh: row: 16 (over z_lo, x, core), col: 16 (over y, z_hi).
Axes of the slice: x: 4, y: 4, z: 8 (z_hi: 4, z_lo: 2; z = z_hi * 2 + z_lo), core: 2. Of those that a mesh axis runs over, the one named last changes fastest.
Arguments:
- pair_density: bfloat16 [4096, 8192], P('col', 'row'), may hold values from -6 to 6
- scale_exp: int32 [4096], replicated, may hold values from -1 to 1
- pair_weight: int32 [4096], replicated, may hold values from 1 to 4
- resident_ids: int32 [512], replicated, may hold values from 0 to 4095, as said below
- diagonal_shift: float32 [8192], replicated, may hold values from 2 to 4
- background: float32 [8192, 8192], P('row', 'col'), as said below
Outputs:
- dielectric: float32 [8192, 8192], P('row', 'col')
- kernel: float32 [4096, 512], P(('col', 'row'))
Inputs may be any that keep to these rules, and one draw needn't show every extreme that they name: `resident_ids`: 512 distinct pair indices. background is symmetric.
All inputs are finite; a program needn't handle non-finite values.
Results may differ from a plain program's by a relative error of at most 0.0003.
Values may be sent and summed in bfloat16 or wider, within the bound.
A program may use at most 64 MiB of HBM per device.

v0:
```python
import math
import jax
import jax.numpy as jnp
from jax import lax
from jax.sharding import PartitionSpec as P

NG = 8192
SWEEPS = 2
damping = 0.5


def from_root(block, axis, owner):
    block = jnp.where(lax.axis_index(axis) == owner, block, jnp.zeros_like(block))
    return lax.psum(block, axis)


def scale_factor(exponent):
    return jnp.where(exponent < 0, 0.5, jnp.where(exponent > 0, 2.0, 1.0)).astype(jnp.float32)


def pair_contract(left_block, right_block):
    return lax.dot_general(
        left_block, right_block, (((0,), (0,)), ((), ())), preferred_element_type=jnp.float32
    )


def shards(pair_density, scale_exp, pair_weight, resident_ids, diagonal_shift, background):
    row_count = lax.axis_size("row")
    col_count = lax.axis_size("col")
    row_index = lax.axis_index("row")
    col_index = lax.axis_index("col")
    pair_dev, row_width = pair_density.shape
    col_width = background.shape[1]
    pair_total = pair_dev * col_count
    norm_scale = 4 * pair_total
    factor = scale_factor(scale_exp)
    own_factor = lax.dynamic_slice_in_dim(factor, col_index * pair_dev, pair_dev)
    scaled = (pair_density.astype(jnp.float32) * own_factor[:, None]).astype(jnp.bfloat16)
    left_all = lax.all_gather(scaled, "col", axis=0, tiled=True)
    pair_rows_all = lax.all_gather(scaled, "row", axis=1, tiled=True)
    right_all = lax.all_to_all(pair_rows_all, "col", split_axis=1, concat_axis=0, tiled=True)
    contracted = pair_contract(left_all, right_all)
    response = contracted / norm_scale
    row_start = row_index * row_width
    col_start = col_index * col_width
    global_rows = row_start + lax.broadcasted_iota(jnp.int32, (row_width, col_width), 0)
    global_cols = col_start + lax.broadcasted_iota(jnp.int32, (row_width, col_width), 1)
    shift_rows = lax.dynamic_slice_in_dim(diagonal_shift, row_start, row_width)
    dielectric = (
        background + response + jnp.where(global_rows == global_cols, shift_rows[:, None], 0.0)
    )
    precond_rows = (
        shift_rows
        + jnp.einsum("pg,pg->g", left_all, left_all, preferred_element_type=jnp.float32)
        / norm_scale
    )
    picked = left_all[resident_ids].astype(jnp.float32) / factor[resident_ids][:, None]
    source_rows = picked.T
    col_ratio = col_count // row_count
    root_row = col_index // col_ratio
    source_cols, precond_cols = (
        from_root(source_rows, "row", root_row),
        from_root(precond_rows, "row", root_row),
    )
    screen_rows = source_rows / precond_rows[:, None]
    screen_cols = source_cols / precond_cols[:, None]
    for sweep_index in range(SWEEPS):
        last_sweep = sweep_index + 1 == SWEEPS
        row_image = lax.psum(
            jnp.dot(dielectric, screen_cols, precision=lax.Precision.HIGHEST), "col"
        )
        if not last_sweep:
            transposed = lax.dot_general(
                dielectric, screen_rows, (((0,), (0,)), ((), ())), precision=lax.Precision.HIGHEST
            )
            col_image = lax.psum(transposed, "row")
            screen_cols = screen_cols + damping * (source_cols - col_image) / precond_cols[:, None]
        screen_rows = screen_rows + damping * (source_rows - row_image) / precond_rows[:, None]
    partial_value = jnp.dot(
        pair_density.astype(jnp.float32), screen_rows, precision=lax.Precision.HIGHEST
    )
    summed = lax.psum_scatter(partial_value, "row", scatter_dimension=0, tiled=True)
    kernel_share = pair_dev // row_count
    weights = lax.dynamic_slice_in_dim(
        pair_weight, col_index * pair_dev + row_index * kernel_share, kernel_share
    ).astype(jnp.float32)
    kernel = weights[:, None] * summed / math.sqrt(NG)
    return (dielectric, kernel)


def solution(mesh):
    return jax.shard_map(
        shards,
        mesh=mesh,
        in_specs=(P("col", "row"), P(), P(), P(), P(), P("row", "col")),
        out_specs=(P("row", "col"), P(("col", "row"), None)),
        check_vma=False,
    )
```

profile of v0, /device:TPU:8, one launch (start us, length us, event | category | flops | bytes accessed | tf_op | source)
XLA Modules:
  0.0 609.8 jit_solution(10730562653668243322)
XLA Ops:
  7.2 0.0 all-gather.5.cloned.1.call-start
  7.2 0.7 select_select_fusion
  7.9 0.1 dynamic_slice.9
  8.0 1.8 multiply_convert_fusion
  9.8 0.0 all-gather.5.cloned.1.call-update
  9.8 0.0 all-gather.3.cloned.1.call-start
  9.8 0.7 all-gather.3.cloned.1.call-update
  10.6 42.7 %all-gather.5.cloned.1.call-done = bf16[256,8192]{1,0:T(8,128)(2,1)} async-done(((bf16[256,512]{1,0:T(8,128)(2,1)}), bf16[256,8192]{1,0:T(8,128)(2,1)}) %all-gather.5.cloned.1.call-update) | async-done | bytes 4194320 | tf_op jit(solution)/shard_map/all_gather | solution.py:40
  53.2 4.6 copy.26
  57.8 0.0 copy-start.1
  57.8 9.7 %all-to-all-start = ((bf16[256,16,512]{2,0,1:T(8,128)(2,1)}), bf16[256,16,512]{2,0,1:T(8,128)(2,1)}, u32[]{:S(2)}, u32[]{:S(2)}) async-start(bf16[256,16,512]{2,0,1:T(8,128)(2,1)} %bitcast.31), calls=%async_computation | async-start | bytes 8388608 | tf_op jit(solution)/shard_map/all_to_all | solution.py:41
  67.6 0.0 all-reduce.7.cloned.1.call-start
  67.6 0.0 copy-done.1
  67.7 3.1 gather_fusion.1
  70.8 132.1 %all-gather.3.cloned.1.call-done = bf16[4096,512]{1,0:T(8,128)(2,1)} async-done(((bf16[256,512]{1,0:T(8,128)(2,1)}), bf16[4096,512]{1,0:T(8,128)(2,1)}) %all-gather.3.cloned.1.call-update) | async-done | bytes 4194320 | tf_op jit(solution)/shard_map/all_gather | solution.py:39
  202.9 4.7 gather_fusion
  207.6 0.0 copy-start.2
  207.6 0.2 copy.14
  207.9 3.2 fusion
  211.1 0.8 broadcast_select_fusion
  211.8 1.2 fusion.16
  213.1 0.0 all-to-all-done
  213.1 0.0 copy-done.2
  213.1 5.8 fusion.2
  218.9 0.0 copy-start.5
  218.9 3.2 fusion.17
  222.1 0.0 all-reduce.7.cloned.1.call-update
  222.1 0.0 all-reduce.5.cloned.1.call-start
  222.2 31.7 %psum.36 = f32[512]{0:T(512)S(1)} all-reduce(f32[512]{0:T(512)S(1)} %get-tuple-element.12), channel_id=1, replica_groups=mesh['row'=16,'col'=16] {'row'}, use_global_device_ids=true, to_apply=%region_1.2 | all-reduce | flops 512 | bytes 4096 | tf_op jit(solution)/shard_map/psum | solution.py:14
  253.9 95.1 %all-reduce.7.cloned.1.call-done = (f32[512,512]{1,0:T(8,128)}, f32[512,512]{1,0:T(8,128)}) async-done(((f32[512,512]{1,0:T(8,128)}, f32[512,512]{1,0:T(8,128)}), (f32[512,512]{1,0:T(8,128)}, f32[512,512]{1,0:T(8,128)})) %all-reduce.7.cloned.1.call-update) | async-done | bytes 2097168 | tf_op jit(solution)/shard_map/psum | solution.py:14
  348.9 0.0 copy-start.3
  348.9 0.0 copy-start.4
  348.9 4.3 fusion.21
  353.3 0.0 copy-done.5
  353.3 0.0 copy-done.3
  353.3 0.0 copy-done.4
  353.3 0.0 copy-start
  353.3 3.1 fusion.7
  356.4 0.0 all-reduce.5.cloned.1.call-update
  356.4 0.0 reduce-scatter.4.cloned.1.call-start
  356.5 177.0 %all-reduce.5.cloned.1.call-done = (f32[512,512]{1,0:T(8,128)}, f32[512,512]{1,0:T(8,128)}) async-done(((f32[512,512]{1,0:T(8,128)}, f32[512,512]{1,0:T(8,128)}), (f32[512,512]{1,0:T(8,128)}, f32[512,512]{1,0:T(8,128)})) %all-reduce.5.cloned.1.call-update) | async-done | bytes 2097168 | tf_op jit(solution)/shard_map/psum | solution.py:69
  533.5 0.0 copy-done
  533.5 2.9 convolution_bitcast_fusion
  536.4 1.0 copy.22
  537.4 0.0 reduce-scatter.4.cloned.1.call-update
  537.4 0.8 dynamic-slice_convert_fusion
  538.2 63.4 %reduce-scatter.4.cloned.1.call-done = f32[16,512]{1,0:T(8,128)} async-done(((f32[256,512]{1,0:T(8,128)}), f32[16,512]{1,0:T(8,128)}) %reduce-scatter.4.cloned.1.call-update) | async-done | bytes 32784
  601.6 0.9 copy.23
  602.5 0.7 copy.15
  (4 shorter events, 0.0 us)
Async XLA Ops:
  7.2 46.1 %all-gather.5.cloned.1.call-start = ((), (), s32[]{:S(2)}) async-start(), calls=%async_computation.3 | async-start | bytes 4456448 | tf_op jit(solution)/shard_map/all_gather | solution.py:40
  9.8 193.1 %all-gather.3.cloned.1.call-start = ((), (), s32[]{:S(2)}) async-start(), calls=%async_computation.2 | async-start | bytes 4456448 | tf_op jit(solution)/shard_map/all_gather | solution.py:39
  57.8 9.8 %copy-start.1 = (s32[512]{0:T(512)S(1)}, s32[512]{0:T(512)}, u32[]{:S(2)}) copy-start(s32[512]{0:T(512)} %param.9) | copy-start | bytes 6148
  57.8 155.2 %all-to-all-start = ((bf16[256,16,512]{2,0,1:T(8,128)(2,1)}), bf16[256,16,512]{2,0,1:T(8,128)(2,1)}, u32[]{:S(2)}, u32[]{:S(2)}) async-start(bf16[256,16,512]{2,0,1:T(8,128)(2,1)} %bitcast.31), calls=%async_computation | async-start | bytes 8388608 | tf_op jit(solution)/shard_map/all_to_all | solution.py:41
  67.6 281.4 %all-reduce.7.cloned.1.call-start = ((), (), s32[]{:S(2)}) async-start(), calls=%async_computation.6 | async-start | bytes 4194304 | tf_op jit(solution)/shard_map/psum | solution.py:14
  207.6 5.4 copy-start.2
  218.9 134.4 %copy-start.5 = (f32[512,512]{1,0:T(8,128)}, f32[512,512]{1,0:T(8,128)S(1)}, u32[]{:S(2)}) copy-start(f32[512,512]{1,0:T(8,128)S(1)} %fusion.2) | copy-start | bytes 3145732
  222.1 311.4 %all-reduce.5.cloned.1.call-start = ((), (), s32[]{:S(2)}) async-start(), calls=%async_computation.5 | async-start | bytes 4194304 | tf_op jit(solution)/shard_map/psum | solution.py:69
  348.9 4.4 copy-start.3
  348.9 4.4 copy-start.4
  353.3 180.2 %copy-start = (bf16[256,512]{1,0:T(8,128)(2,1)S(1)}, bf16[256,512]{1,0:T(8,128)(2,1)}, u32[]{:S(2)}) copy-start(bf16[256,512]{1,0:T(8,128)(2,1)} %param.6) | copy-start | bytes 786436
  356.4 245.2 %reduce-scatter.4.cloned.1.call-start = ((), (), s32[]{:S(2)}) async-start(), calls=%async_computation.4 | async-start | bytes 557056
Sparse Core Ops, SparseCore 0:
  10.4 42.7 all-gather.4
  56.2 146.6 all-gather.2
  222.3 126.6 all-reduce.6
  356.5 176.8 all-reduce.4
  537.5 64.0 reduce-scatter.3
where the time goes:
time: 610 us
  waiting for transfers between devices  511 us (84%)
  blocking collectives  31.7 us (5%)
  matrix products  19.4 us (3%)
  local copies, waits for them, and re-layouts  15.4 us (3%)
  between operations  13.9 us (2%)
  starting transfers between devices  9.95 us (2%)
  other arithmetic  8.49 us (1%)
    psum x1, waiting for transfers between devices, shards(): lax.psum(jnp.dot(dielectric, screen_cols, precision=lax.Precision.HIGHEST...  177 us
    all_gather x1, waiting for transfers between devices, shards(): left_all = lax.all_gather(scaled, 'col', axis=0, tiled=True)  132 us
    psum x1, waiting for transfers between devices, from_root(): return lax.psum(block, axis)  95.1 us
    unnamed x6, waiting for transfers between devices  64.2 us
    all_gather x1, waiting for transfers between devices, shards(): pair_rows_all = lax.all_gather(scaled, 'row', axis=1, tiled=True)  42.7 us
    psum x1, blocking collectives, from_root(): return lax.psum(block, axis)  31.7 us
  transfers between devices with their start and end apart: 6, of which 5 were waited for; matrix products, arithmetic and copies ran while one was open for 3% of the time, Pallas kernels for 0%

commit v1 on v0

--- a/solution.py
+++ b/solution.py
@@ -11,7 +11,7 @@
 
 def from_root(block, axis, owner):
     block = jnp.where(lax.axis_index(axis) == owner, block, jnp.zeros_like(block))
-    return lax.psum(block, axis)
+    return jnp.sum(lax.all_gather(block, axis), axis=0)
 
 
 def scale_factor(exponent):

time: 610 us -> 703 us (1.15)
  waiting for transfers between devices: 511 us -> 608 us
  blocking collectives: 31.7 us -> 18.2 us
  other arithmetic: 8.49 us -> 17.1 us
    all_to_all x1, waiting for transfers between devices: 0.01 us -> 137 us  [shards(): lax.all_to_all(pair_rows_all, 'col', split_axis=1, concat_axis=0, tiled=T...]
    all_gather x1, waiting for transfers between devices: 132 us -> 75.4 us  [shards(): left_all = lax.all_gather(scaled, 'col', axis=0, tiled=True)]
    psum x1 -> x0, blocking collectives: 31.7 us -> none  [from_root(): return lax.psum(block, axis)]
    psum x1, waiting for transfers between devices: 95.1 us -> 115 us  [shards(): col_image = lax.psum(transposed, 'row')]
    all_gather x0 -> x1, blocking collectives: none -> 18.2 us  [from_root(): return jnp.sum(lax.all_gather(block, axis), axis=0)]
    reduce_sum x0 -> x2, other arithmetic: none -> 7.96 us  [from_root(): return jnp.sum(lax.all_gather(block, axis), axis=0)]
    unnamed x6 -> x7, waiting for transfers between devices: 64.2 us -> 64.2 us
  transfers between devices with their start and end apart: 6 -> 7, of which waited for: 5 -> 7; matrix products, arithmetic and copies ran while one was open for 3% -> 6% of each run, Pallas kernels for 0% -> 0%
where the time goes in v1:
time: 703 us
  waiting for transfers between devices  608 us (86%)
  matrix products  19.4 us (3%)
  blocking collectives  18.2 us (3%)
  other arithmetic  17.1 us (2%)
  local copies, waits for them, and re-layouts  15.4 us (2%)
  between operations  14.2 us (2%)
  starting transfers between devices  9.86 us (1%)
    psum x1, waiting for transfers between devices, shards(): lax.psum(jnp.dot(dielectric, screen_cols, precision=lax.Precision.HIGHEST...  178 us
    all_to_all x1, waiting for transfers between devices, shards(): lax.all_to_all(pair_rows_all, 'col', split_axis=1, concat_axis=0, tiled=T...  137 us
    psum x1, waiting for transfers between devices, shards(): col_image = lax.psum(transposed, 'row')  115 us
    all_gather x1, waiting for transfers between devices, shards(): left_all = lax.all_gather(scaled, 'col', axis=0, tiled=True)  75.4 us
    unnamed x7, waiting for transfers between devices  64.2 us
    all_gather x1, waiting for transfers between devices, shards(): pair_rows_all = lax.all_gather(scaled, 'row', axis=1, tiled=True)  36 us
    all_gather x1, blocking collectives, from_root(): return jnp.sum(lax.all_gather(block, axis), axis=0)  18.2 us
  transfers between devices with their start and end apart: 7, of which 7 were waited for; matrix products, arithmetic and copies ran while one was open for 6% of the time, Pallas kernels for 0%

profile of v1, /device:TPU:8, one launch (start us, length us, event | category | flops | bytes accessed | tf_op | source)
XLA Modules:
  0.0 702.6 jit_solution(9417552925331624193)
XLA Ops:
  7.2 0.0 all-gather.7.cloned.1.call-start
  7.2 0.7 select_select_fusion
  7.9 0.1 dynamic_slice.9
  8.0 1.8 multiply_convert_fusion
  9.8 0.0 all-gather.7.cloned.1.call-update
  9.8 0.0 all-gather.9.cloned.1.call-start
  9.8 0.7 all-gather.9.cloned.1.call-update
  10.6 0.0 all-gather.11.cloned.1.call-start
  10.6 0.7 compare_select_fusion
  11.3 3.1 gather_fusion.1
  14.4 75.4 %all-gather.7.cloned.1.call-done = bf16[4096,512]{1,0:T(8,128)(2,1)} async-done(((bf16[256,512]{1,0:T(8,128)(2,1)}), bf16[4096,512]{1,0:T(8,128)(2,1)}) %all-gather.7.cloned.1.call-update) | async-done | bytes 4194320 | tf_op jit(solution)/shard_map/all_gather | solution.py:39
  89.8 4.7 gather_fusion
  94.6 0.2 copy.14
  94.8 1.2 fusion.16
  96.0 0.0 all-gather.11.cloned.1.call-update
  96.0 36.0 %all-gather.9.cloned.1.call-done = bf16[256,8192]{1,0:T(8,128)(2,1)} async-done(((bf16[256,512]{1,0:T(8,128)(2,1)}), bf16[256,8192]{1,0:T(8,128)(2,1)}) %all-gather.9.cloned.1.call-update) | async-done | bytes 4194320 | tf_op jit(solution)/shard_map/all_gather | solution.py:40
  132.0 4.6 copy.26
  136.6 9.6 %all-to-all-start = ((bf16[256,16,512]{2,0,1:T(8,128)(2,1)}), bf16[256,16,512]{2,0,1:T(8,128)(2,1)}, u32[]{:S(2)}, u32[]{:S(2)}) async-start(bf16[256,16,512]{2,0,1:T(8,128)(2,1)} %bitcast.34), calls=%async_computation | async-start | bytes 8388608 | tf_op jit(solution)/shard_map/all_to_all | solution.py:41
  146.2 0.0 copy-start.1
  146.2 0.0 all-reduce.4.cloned.1.call-start
  146.3 3.2 fusion
  149.5 0.8 broadcast_select_fusion
  150.3 136.9 %all-to-all-done = bf16[256,16,512]{2,0,1:T(8,128)(2,1)} async-done(((bf16[256,16,512]{2,0,1:T(8,128)(2,1)}), bf16[256,16,512]{2,0,1:T(8,128)(2,1)}, u32[]{:S(2)}, u32[]{:S(2)}) %all-to-all-start) | async-done | bytes 4194336 | tf_op jit(solution)/shard_map/all_to_all | solution.py:41
  287.2 0.0 copy-done.1
  287.2 6.0 fusion.2
  293.2 0.0 copy-start.2
  293.2 3.2 fusion.17
  296.4 0.0 all-reduce.4.cloned.1.call-update
  296.5 0.0 all-reduce.6.cloned.1.call-start
  296.5 18.2 %all-gather.2 = f32[16,1,512]{2,1,0:T(1,128)S(1)} all-gather(f32[1,1,512]{2,1,0:T(1,128)S(1)} %bitcast.36), channel_id=3, replica_groups=mesh['row'=16,'col'=16] {'row'}, dimensions={0}, use_global_device_ids=true | all-gather | bytes 34816 | tf_op jit(solution)/shard_map/all_gather | solution.py:14
  314.7 3.3 all-gather.11.cloned.1.call-done
  318.1 7.9 %reduce_sum.18 = f32[512,512]{1,0:T(8,128)S(1)} reduce(f32[16,512,512]{2,1,0:T(8,128)} %bitcast.33, f32[]{:T(128)} %constant.49.clone.1), dimensions={0}, to_apply=%region_0.1 | reduce | flops 3932160 | bytes 17825796 | tf_op jit(solution)/shard_map/reduce_sum | solution.py:14
  326.0 2.9 fusion.21
  328.9 0.0 copy-start
  329.0 115.1 %all-reduce.4.cloned.1.call-done = f32[512,512]{1,0:T(8,128)} async-done(((f32[512,512]{1,0:T(8,128)}), f32[512,512]{1,0:T(8,128)}) %all-reduce.4.cloned.1.call-update) | async-done | bytes 1048592 | tf_op jit(solution)/shard_map/psum | solution.py:76
  444.0 0.0 copy-done.2
  444.0 4.3 fusion.7
  448.4 0.0 all-reduce.6.cloned.1.call-update
  448.4 0.0 reduce-scatter.4.cloned.1.call-start
  448.5 177.5 %all-reduce.6.cloned.1.call-done = (f32[512,512]{1,0:T(8,128)}, f32[512,512]{1,0:T(8,128)}) async-done(((f32[512,512]{1,0:T(8,128)}, f32[512,512]{1,0:T(8,128)}), (f32[512,512]{1,0:T(8,128)}, f32[512,512]{1,0:T(8,128)})) %all-reduce.6.cloned.1.call-update) | async-done | bytes 2097168 | tf_op jit(solution)/shard_map/psum | solution.py:69
  626.0 0.0 copy-done
  626.0 2.9 convolution_bitcast_fusion
  628.9 1.0 copy.22
  629.9 0.0 reduce-scatter.4.cloned.1.call-update
  629.9 0.8 dynamic-slice_convert_fusion
  630.7 63.4 %reduce-scatter.4.cloned.1.call-done = f32[16,512]{1,0:T(8,128)} async-done(((f32[256,512]{1,0:T(8,128)}), f32[16,512]{1,0:T(8,128)}) %reduce-scatter.4.cloned.1.call-update) | async-done | bytes 32784
  694.1 0.9 copy.23
  695.1 0.7 copy.15
  (4 shorter events, 0.1 us)
Async XLA Ops:
  7.2 82.7 %all-gather.7.cloned.1.call-start = ((), (), s32[]{:S(2)}) async-start(), calls=%async_computation.2 | async-start | bytes 4456448 | tf_op jit(solution)/shard_map/all_gather | solution.py:39
  9.8 122.2 %all-gather.9.cloned.1.call-start = ((), (), s32[]{:S(2)}) async-start(), calls=%async_computation.3 | async-start | bytes 4456448 | tf_op jit(solution)/shard_map/all_gather | solution.py:40
  10.6 307.5 %all-gather.11.cloned.1.call-start = ((), (), s32[]{:S(2)}) async-start(), calls=%async_computation.5 | async-start | bytes 17825792 | tf_op jit(solution)/shard_map/all_gather | solution.py:14
  136.6 150.6 %all-to-all-start = ((bf16[256,16,512]{2,0,1:T(8,128)(2,1)}), bf16[256,16,512]{2,0,1:T(8,128)(2,1)}, u32[]{:S(2)}, u32[]{:S(2)}) async-start(bf16[256,16,512]{2,0,1:T(8,128)(2,1)} %bitcast.34), calls=%async_computation | async-start | bytes 8388608 | tf_op jit(solution)/shard_map/all_to_all | solution.py:41
  146.2 140.9 %copy-start.1 = (f32[512,512]{1,0:T(8,128)S(1)}, f32[512,512]{1,0:T(8,128)}, u32[]{:S(2)}) copy-start(f32[512,512]{1,0:T(8,128)} %param.11) | copy-start | bytes 3145732
  146.2 297.8 %all-reduce.4.cloned.1.call-start = ((), (), s32[]{:S(2)}) async-start(), calls=%async_computation.4 | async-start | bytes 2097152 | tf_op jit(solution)/shard_map/psum | solution.py:76
  293.2 150.9 %copy-start.2 = (f32[512,512]{1,0:T(8,128)}, f32[512,512]{1,0:T(8,128)S(1)}, u32[]{:S(2)}) copy-start(f32[512,512]{1,0:T(8,128)S(1)} %fusion.2) | copy-start | bytes 3145732
  296.5 329.6 %all-reduce.6.cloned.1.call-start = ((), (), s32[]{:S(2)}) async-start(), calls=%async_computation.7 | async-start | bytes 4194304 | tf_op jit(solution)/shard_map/psum | solution.py:69
  328.9 297.1 %copy-start = (bf16[256,512]{1,0:T(8,128)(2,1)S(1)}, bf16[256,512]{1,0:T(8,128)(2,1)}, u32[]{:S(2)}) copy-start(bf16[256,512]{1,0:T(8,128)(2,1)} %param.6) | copy-start | bytes 786436
  448.4 245.7 %reduce-scatter.4.cloned.1.call-start = ((), (), s32[]{:S(2)}) async-start(), calls=%async_computation.6 | async-start | bytes 557056
Sparse Core Ops, SparseCore 0:
  11.0 78.7 all-gather.6
  92.2 39.7 all-gather.8
  133.8 184.1 all-gather.10
  320.6 123.4 all-reduce.3
  448.5 177.4 all-reduce.5
  630.1 64.0 reduce-scatter.3
